TPU v7x, 512 devices: a whole 4x8x8 slice. The times are simulated.
512 devices in a mesh: ctx: 16 (over y, core), nbr: 8 (over z), tp: 4 (over x).
Axes of the slice: x: 4, y: 8, z: 8, core: 2. Of those that a mesh axis runs over, the one named last changes fastest.
Arguments:
- hidden: bfloat16 [32768, 4096], P(('ctx', 'nbr'), 'tp'), may hold values from -6 to 6
- queries: bfloat16 [32768, 2048], P(('ctx', 'nbr'), 'tp'), may hold values from -6 to 6
- key_weight_matrix: bfloat16 [768, 2048], P('ctx', 'tp'), may hold values from -0.21875 to 0.21875
- value_weight_matrix: bfloat16 [768, 2048], P('ctx', 'tp'), may hold values from -0.21875 to 0.21875
- w_out: bfloat16 [2048, 4096], P('ctx', 'tp'), may hold values from -0.125 to 0.125
- neighbour_embed: bfloat16 [1024, 128, 768], P(('ctx', 'nbr')), may hold values from -6 to 6
- neighbour_ids: int32 [1024, 128], P(('ctx', 'nbr')), may hold values from 0 to 127999, as said below
- neighbour_count: int32 [512], P(('ctx', 'nbr')), may hold values from 0 to 2, as said below
- slot_seq: int32 [128, 8], replicated, may hold values from 0 to 7, as said below
- cond_keys: bfloat16 [32768, 768], P(('ctx', 'nbr'), 'tp'), may hold values from -6 to 6
- cond_values: bfloat16 [32768, 768], P(('ctx', 'nbr'), 'tp'), may hold values from -6 to 6
- enc_gain: bfloat16 [768], replicated, may hold values from 0.5 to 1.5
- enc_query: bfloat16 [768, 768], P(None, 'tp'), may hold values from -0.21875 to 0.21875
- enc_out: bfloat16 [768, 768], P('tp'), may hold values from -0.21875 to 0.21875
- final_gain: bfloat16 [768], replicated, may hold values from 0.5 to 1.5
Outputs:
- output: bfloat16 [32768, 4096], P(('ctx', 'nbr'), 'tp')
Inputs may be any that keep to these rules, and one draw needn't show every extreme that they name: `neighbour_ids`: every neighbour's ids are nonzero up to a length of at least 32 tokens and 0 after it. `slot_seq`: each row is a permutation of 0 to 7. `neighbour_count`: the last stretch of every block of positions has at least one valid neighbour.
All inputs are finite; a program needn't handle non-finite values.
Results may differ from a plain program's by a relative error of at most 0.0075.
Values may be sent and summed in bfloat16 or wider, within the bound.
A program may use at most 64 MiB of HBM per device.

v0:
```python
import jax
import jax.numpy as jnp
from jax import lax
from jax.sharding import PartitionSpec as P

HEAD_WIDTH = 128
EHD = 64
STRETCH_TOKENS = 64
NEIGHBOUR_TOKENS = 128
NEIGHBOUR_COUNT = 2
EPSILON = 1e-06


def from_behind(block, axis, distance):
    devices = range(lax.axis_size(axis))
    route = [(i - distance, i) for i in devices if i - distance in devices]
    return lax.ppermute(block, axis, route)


def row_rscale(matrix):
    return lax.rsqrt(jnp.mean(matrix * matrix, axis=-1, keepdims=True) + EPSILON)


def masked_attend(query_rows, key_rows, value_rows, allowed, score_scale):
    scores = (
        jnp.einsum("bqhd,bkhd->bhqk", query_rows, key_rows, preferred_element_type=jnp.float32)
        * score_scale
    )
    allowed_map = allowed[:, None, None, :]
    highest = jnp.max(jnp.where(allowed_map, scores, -1e30), axis=-1, keepdims=True)
    raised = jnp.where(allowed_map, jnp.exp(scores - highest), 0.0)
    totals = jnp.sum(raised, axis=-1, keepdims=True)
    anyone = jnp.any(allowed, axis=-1)[:, None, None, None]
    weights = (raised / jnp.where(anyone, totals, 1.0)).astype(jnp.bfloat16)
    return jnp.einsum(
        "bhqk,bkhd->bqhd", weights, value_rows, preferred_element_type=jnp.float32
    ).astype(jnp.bfloat16)


def per_device(
    hidden,
    queries,
    key_weight_matrix,
    value_weight_matrix,
    w_out,
    neighbour_embed,
    neighbour_ids,
    neighbour_count,
    slot_seq,
    cond_keys,
    cond_values,
    enc_gain,
    enc_query,
    enc_out,
    final_gain,
):
    tok_rows = hidden.shape[0]
    head_cols = queries.shape[1]
    heads_here = head_cols // HEAD_WIDTH
    block_seqs = neighbour_embed.shape[0]
    enc_width = neighbour_embed.shape[2]
    enc_cols = enc_query.shape[1]
    owners = lax.axis_size("nbr")
    tp_count = lax.axis_size("tp")
    per_owner = block_seqs // owners
    group_size = tok_rows // STRETCH_TOKENS
    quarter = NEIGHBOUR_TOKENS // tp_count
    ctx_place = lax.axis_index("ctx")
    nbr_place = lax.axis_index("nbr")
    tp_place = lax.axis_index("tp")
    table = lax.dynamic_slice_in_dim(slot_seq, ctx_place * owners, owners, 0)
    my_row = lax.dynamic_index_in_dim(table, nbr_place, 0, keepdims=False)
    send_stretches = (my_row // NEIGHBOUR_COUNT).reshape(owners, per_owner)
    sent_keys = jnp.take(
        cond_keys.reshape(group_size, STRETCH_TOKENS, enc_cols), send_stretches, axis=0
    )
    sent_values = jnp.take(
        cond_values.reshape(group_size, STRETCH_TOKENS, enc_cols), send_stretches, axis=0
    )
    got_keys, got_values = (
        lax.all_to_all(sent_keys, "nbr", split_axis=0, concat_axis=0, tiled=True),
        lax.all_to_all(sent_values, "nbr", split_axis=0, concat_axis=0, tiled=True),
    )
    wide_embed = neighbour_embed.astype(jnp.float32)
    own_rows = lax.dynamic_slice_in_dim(wide_embed, tp_place * quarter, quarter, 1)
    gain_wide = enc_gain.astype(jnp.float32)
    heads_enc = enc_cols // EHD
    normed = (wide_embed * row_rscale(wide_embed) * gain_wide).astype(jnp.bfloat16)
    enc_q = jnp.dot(
        normed.reshape(block_seqs * NEIGHBOUR_TOKENS, enc_width),
        enc_query,
        preferred_element_type=jnp.float32,
    ).astype(jnp.bfloat16)
    enc_q = enc_q.reshape(block_seqs, NEIGHBOUR_TOKENS, heads_enc, EHD)
    key_rows = got_keys.reshape(block_seqs, STRETCH_TOKENS, heads_enc, EHD)
    value_rows = got_values.reshape(block_seqs, STRETCH_TOKENS, heads_enc, EHD)
    mixed = masked_attend(
        enc_q,
        key_rows,
        value_rows,
        jnp.ones((block_seqs, STRETCH_TOKENS), dtype=bool),
        EHD ** (-0.5),
    )
    ordered = (
        mixed.reshape(block_seqs, tp_count, quarter, enc_cols)
        .transpose(1, 0, 2, 3)
        .reshape(tp_count * block_seqs * quarter, enc_cols)
    )
    term = jnp.dot(ordered, enc_out, preferred_element_type=jnp.float32)
    summed = (
        lax.psum_scatter(term.astype(jnp.bfloat16), "tp", scatter_dimension=0, tiled=True)
        .astype(jnp.float32)
        .reshape(block_seqs, quarter, enc_width)
    )
    updated = own_rows + summed
    encoded = (updated * row_rscale(updated) * final_gain.astype(jnp.float32)).astype(jnp.bfloat16)
    key_full, value_full = (
        lax.all_gather(key_weight_matrix, "ctx", axis=0, tiled=True),
        lax.all_gather(value_weight_matrix, "ctx", axis=0, tiled=True),
    )
    both_weights = jnp.concatenate([key_full, value_full], axis=1)
    back = lax.all_to_all(
        encoded.reshape(owners, per_owner, quarter, enc_width),
        "nbr",
        split_axis=0,
        concat_axis=0,
        tiled=True,
    )
    slot_kv = jnp.dot(
        lax.all_gather(back.reshape(block_seqs, quarter, enc_width), "tp", axis=1, tiled=True),
        both_weights,
        preferred_element_type=jnp.float32,
    ).astype(jnp.bfloat16)
    matches = my_row[:, None] == jnp.arange(block_seqs, dtype=jnp.int32)[None, :]
    inverse = jnp.sum(
        jnp.where(matches, jnp.arange(block_seqs, dtype=jnp.int32)[:, None], 0), axis=0
    )
    stretch_kv = jnp.take(slot_kv, inverse, axis=0).reshape(
        group_size, NEIGHBOUR_COUNT * NEIGHBOUR_TOKENS, 2 * head_cols
    )
    live = (
        jnp.arange(NEIGHBOUR_COUNT, dtype=jnp.int32)[None, :, None] < neighbour_count[:, None, None]
    ) & (neighbour_ids.reshape(group_size, NEIGHBOUR_COUNT, NEIGHBOUR_TOKENS) != 0)
    stretch_live = live.reshape(group_size, NEIGHBOUR_COUNT * NEIGHBOUR_TOKENS)

    def split_keys(kv_block):
        return kv_block[..., :head_cols].reshape(
            kv_block.shape[0], NEIGHBOUR_COUNT * NEIGHBOUR_TOKENS, heads_here, HEAD_WIDTH
        )

    def split_values(kv_block):
        return kv_block[..., head_cols:].reshape(
            kv_block.shape[0], NEIGHBOUR_COUNT * NEIGHBOUR_TOKENS, heads_here, HEAD_WIDTH
        )

    score_scale = HEAD_WIDTH ** (-0.5)
    live_mark = stretch_live.astype(jnp.bfloat16)
    before_kv, before_mark = from_behind(
        (stretch_kv[group_size - 1 :], live_mark[group_size - 1 :]), ("ctx", "nbr"), 1
    )
    then_kv = jnp.concatenate([before_kv, stretch_kv[:-1]], axis=0)
    then_live = jnp.concatenate([before_mark > 0.5, stretch_live[:-1]], axis=0)
    grouped = queries.reshape(group_size, STRETCH_TOKENS, heads_here, HEAD_WIDTH)
    early_rows = masked_attend(
        grouped[:, : STRETCH_TOKENS - 1],
        split_keys(then_kv),
        split_values(then_kv),
        then_live,
        score_scale,
    )
    last_rows = masked_attend(
        grouped[:, STRETCH_TOKENS - 1 :],
        split_keys(stretch_kv),
        split_values(stretch_kv),
        stretch_live,
        score_scale,
    )
    attended = jnp.concatenate([early_rows, last_rows], axis=1).reshape(tok_rows, head_cols)
    all_heads = lax.all_gather(attended, "tp", axis=1, tiled=True)
    mixed_out = jnp.dot(
        all_heads,
        lax.all_gather(w_out, "ctx", axis=0, tiled=True),
        preferred_element_type=jnp.float32,
    )
    return (hidden.astype(jnp.float32) + mixed_out).astype(jnp.bfloat16)


def solution(mesh):
    in_specs = (
        P(("ctx", "nbr"), "tp"),
        P(("ctx", "nbr"), "tp"),
        P("ctx", "tp"),
        P("ctx", "tp"),
        P("ctx", "tp"),
        P(("ctx", "nbr"), None, None),
        P(("ctx", "nbr"), None),
        P(("ctx", "nbr")),
        P(),
        P(("ctx", "nbr"), "tp"),
        P(("ctx", "nbr"), "tp"),
        P(),
        P(None, "tp"),
        P("tp", None),
        P(),
    )
    out_specs = P(("ctx", "nbr"), "tp")
    return jax.shard_map(
        per_device, mesh=mesh, in_specs=in_specs, out_specs=out_specs, check_vma=False
    )
```

profile of v0, /device:TPU:1, one launch (start us, length us, event | category | flops | bytes accessed | tf_op | source)
XLA Modules:
  0.0 219.3 jit_solution(40663971459019656)
XLA Ops:
  6.5 1.0 dynamic-slice_reduce_fusion
  7.6 1.0 copy.52
  8.6 1.0 copy.55
  9.6 0.6 gather_fusion.1
  10.2 0.6 gather_fusion.2
  10.7 0.9 fusion.37
  11.7 10.9 %all-to-all-start.1 = ((bf16[8,1,64,192]{3,2,1,0:T(8,128)(2,1)}), bf16[8,1,64,192]{3,2,1,0:T(8,128)(2,1)S(1)}, u32[]{:S(2)}, u32[]{:S(2)}) async-start(bf16[8,1,64,192]{3,2,1,0:T(8,128)(2,1)} %get-tuple-element.14), calls=%async_computation.1 | async-start | bytes 524288 | tf_op jit(solution)/shard_map/all_to_all | solution.py:81
  22.5 0.4 multiply_reduce_fusion
  23.0 0.4 multiply_convert_fusion
  23.4 0.1 copy-done.5
  23.5 0.7 fusion.20
  24.2 8.7 %all-to-all-done.1 = bf16[8,1,64,192]{3,2,1,0:T(8,128)(2,1)S(1)} async-done(((bf16[8,1,64,192]{3,2,1,0:T(8,128)(2,1)}), bf16[8,1,64,192]{3,2,1,0:T(8,128)(2,1)S(1)}, u32[]{:S(2)}, u32[]{:S(2)}) %all-to-all-start.1) | async-done | bytes 196640 | tf_op jit(solution)/shard_map/all_to_all | solution.py:81
  32.9 3.4 %all-to-all-start = ((bf16[8,1,64,192]{3,2,1,0:T(8,128)(2,1)}), bf16[8,1,64,192]{3,2,1,0:T(8,128)(2,1)S(1)}, u32[]{:S(2)}, u32[]{:S(2)}) async-start(bf16[8,1,64,192]{3,2,1,0:T(8,128)(2,1)} %get-tuple-element.15), calls=%async_computation | async-start | bytes 524288 | tf_op jit(solution)/shard_map/all_to_all | solution.py:82
  36.4 0.2 copy.57
  36.6 0.5 fusion.67
  37.0 1.2 convolution_multiply_fusion.1
  38.2 7.4 %all-to-all-done = bf16[8,1,64,192]{3,2,1,0:T(8,128)(2,1)S(1)} async-done(((bf16[8,1,64,192]{3,2,1,0:T(8,128)(2,1)}), bf16[8,1,64,192]{3,2,1,0:T(8,128)(2,1)S(1)}, u32[]{:S(2)}, u32[]{:S(2)}) %all-to-all-start) | async-done | bytes 196640 | tf_op jit(solution)/shard_map/all_to_all | solution.py:82
  45.7 0.2 copy.54
  45.9 1.7 fusion.21
  47.6 0.7 copy.60
  48.3 0.7 reshape.309
  49.0 1.7 convolution_convert_fusion.1
  50.8 2.0 convert_element_type.61
  52.7 27.2 %reduce-scatter.2.cloned.1.call-done = bf16[256,768]{1,0:T(8,128)(2,1)} async-done(((bf16[1024,768]{1,0:T(8,128)(2,1)}), bf16[256,768]{1,0:T(8,128)(2,1)}) %reduce-scatter.2.cloned.1.call-update) | async-done | bytes 393232 | tf_op jit(solution)/shard_map/reduce_scatter | solution.py:111
  79.9 1.5 multiply_reduce_fusion.1
  81.4 1.4 fusion.33
  82.8 18.6 %all_to_all.15 = bf16[8,1,32,768]{3,2,1,0:T(8,128)(2,1)} all-to-all(bf16[8,1,32,768]{3,2,1,0:T(8,128)(2,1)S(1)} %fusion.33), channel_id=1, replica_groups=mesh['ctx'=16,'nbr'=8,'tp'=4] {'nbr'}, dimensions={0} | all-to-all | bytes 786432 | tf_op jit(solution)/shard_map/all_to_all | solution.py:122
  101.5 0.7 all-gather.7.cloned.1.call-update
  102.3 0.1 lt.62
  102.4 0.2 and_reduce_fusion
  102.7 2.2 %collective-permute-start.1 = (bf16[1,256]{1,0:T(2,128)(2,1)S(1)}, bf16[1,256]{1,0:T(2,128)(2,1)S(1)}, u32[]{:S(2)}, u32[]{:S(2)}) collective-permute-start(bf16[1,256]{1,0:T(2,128)(2,1)S(1)} %slice_convert_fusion), channel_id=1, source_target_pairs={{0,4},{4,8},{8,12},{12,16},{16,20},{20,24},{24,28},{28,32},{32,36}... | collective-permute-start | bytes 1544 | tf_op jit(solution)/shard_map/ppermute | solution.py:17
  105.0 0.1 select_reduce_fusion.2
  105.1 0.1 reduce_sum.64
  105.2 0.1 copy.68
  105.5 23.3 %all_gather.16 = bf16[768,512]{1,0:T(8,128)(2,1)S(1)} all-gather(bf16[48,512]{1,0:T(8,128)(2,1)S(1)} %copy-done.7), channel_id=1, replica_groups=mesh['ctx'=16,'nbr'=8,'tp'=4] {'ctx'}, dimensions={0}, use_global_device_ids=true | all-gather | bytes 835584 | tf_op jit(solution)/shard_map/all_gather | solution.py:118
  128.8 17.3 %all_gather.17 = bf16[768,512]{1,0:T(8,128)(2,1)S(1)} all-gather(bf16[48,512]{1,0:T(8,128)(2,1)S(1)} %copy-done.8), channel_id=1, replica_groups=mesh['ctx'=16,'nbr'=8,'tp'=4] {'ctx'}, dimensions={0}, use_global_device_ids=true | all-gather | bytes 835584 | tf_op jit(solution)/shard_map/all_gather | solution.py:119
  146.1 0.1 reduce_or.27
  146.2 0.1 reduce_or.28
  146.3 0.1 fusion.66
  146.5 4.5 %convolution_convert_fusion = bf16[8,128,1024]{2,1,0:T(8,128)(2,1)} fusion(bf16[768,512]{1,0:T(8,128)(2,1)S(1)} %all_gather.17, bf16[768,512]{1,0:T(8,128)(2,1)S(1)} %all_gather.16, bf16[8,1,128,768]{3,2,0,1:T(8,128)(2,1)} %all-gather.9.cloned.1.call-done), kind=kOutput, calls=%fused_computation.12 | convolution fusion | flops 1614807040 | bytes 5242880 | tf_op jit(solution)/shard_map/dot_general | solution.py:129
  151.0 2.3 %gather_fusion = bf16[8,128,1024]{2,1,0:T(8,128)(2,1)S(1)} fusion(bf16[8,128,1024]{2,1,0:T(8,128)(2,1)} %convolution_convert_fusion, s32[1024]{0:T(1024)S(1)} %pad_clamp_fusion), kind=kCustom, calls=%fused_computation.2 | custom fusion | bytes 4194336 | tf_op jit(solution)/shard_map/jit(_take)/gather | solution.py:138
  153.3 0.3 broadcast_select_fusion
  153.6 1.3 copy-done.2
  154.9 1.0 copy.63
  155.9 2.1 collective-permute-start
  158.0 0.3 bitcast_select_fusion
  158.3 1.3 slice_bitcast_fusion
  159.6 0.4 fusion.27
  159.9 0.2 fusion.70
  160.3 0.7 slice-done
  161.0 0.7 copy.64
  161.7 1.5 copy.80
  163.2 0.4 fusion.40
  163.6 6.0 %collective-permute-done = bf16[1,256,1024]{1,2,0:T(8,128)(2,1)} collective-permute-done((bf16[1,256,1024]{1,2,0:T(8,128)(2,1)}, bf16[1,256,1024]{1,2,0:T(8,128)(2,1)}, u32[]{:S(2)}, u32[]{:S(2)}) %collective-permute-start) | collective-permute-done | bytes 524320 | tf_op jit(solution)/shard_map/ppermute | solution.py:17
  169.5 2.1 pad_maximum_fusion
  171.7 0.3 convolution_multiply_fusion
  172.0 0.4 fusion.71
  172.5 0.5 copy-done.4
  172.9 1.8 fusion.22
  174.9 0.2 copy.70
  175.1 0.7 copy.117
  175.8 3.3 %all-gather.7.cloned.1.call-done = bf16[2048,1024]{1,0:T(8,128)(2,1)} async-done(((bf16[128,1024]{1,0:T(8,128)(2,1)}), bf16[2048,1024]{1,0:T(8,128)(2,1)}) %all-gather.7.cloned.1.call-update) | async-done | bytes 4194320 | tf_op jit(solution)/shard_map/all_gather | solution.py:182
  179.1 29.1 %all-gather.5.cloned.1.call-done = bf16[256,2048]{1,0:T(8,128)(2,1)} async-done(((bf16[256,512]{1,0:T(8,128)(2,1)}), bf16[256,2048]{1,0:T(8,128)(2,1)}) %all-gather.5.cloned.1.call-update) | async-done | bytes 1048592 | tf_op jit(solution)/shard_map/all_gather | solution.py:179
  208.2 4.6 %fusion.18 = bf16[256,1024]{1,0:T(8,128)(2,1)} fusion(bf16[256,2048]{1,0:T(8,128)(2,1)} %all-gather.5.cloned.1.call-done, bf16[2048,1024]{1,0:T(8,128)(2,1)} %all-gather.7.cloned.1.call-done, bf16[256,1024]{1,0:T(8,128)(2,1)S(1)} %copy-done.12), kind=kOutput, calls=%fused_computation.27 | convolution fusion | flops 1074528256 | bytes 6291456 | tf_op jit(solution)/shard_map/dot_general | solution.py:180
  (69 shorter events, 1.2 us)
Async XLA Ops:
  6.5 42.4 %copy-start = (bf16[192,768]{1,0:T(8,128)(2,1)S(1)}, bf16[192,768]{1,0:T(8,128)(2,1)}, u32[]{:S(2)}) copy-start(bf16[192,768]{1,0:T(8,128)(2,1)} %param.30) | copy-start | bytes 884740
  6.5 16.0 %copy-start.1 = (bf16[8,128,768]{2,1,0:T(8,128)(2,1)S(1)}, bf16[8,128,768]{2,1,0:T(8,128)(2,1)}, u32[]{:S(2)}) copy-start(bf16[8,128,768]{2,1,0:T(8,128)(2,1)} %param.22) | copy-start | bytes 4718596
  9.6 13.3 %copy-start.10 = (bf16[768]{0:T(1024)(128)(2,1)S(1)}, bf16[768]{0:T(1024)(128)(2,1)}, u32[]{:S(2)}) copy-start(bf16[768]{0:T(1024)(128)(2,1)} %param.28) | copy-start | bytes 4612
  11.7 21.2 %all-to-all-start.1 = ((bf16[8,1,64,192]{3,2,1,0:T(8,128)(2,1)}), bf16[8,1,64,192]{3,2,1,0:T(8,128)(2,1)S(1)}, u32[]{:S(2)}, u32[]{:S(2)}) async-start(bf16[8,1,64,192]{3,2,1,0:T(8,128)(2,1)} %get-tuple-element.14), calls=%async_computation.1 | async-start | bytes 524288 | tf_op jit(solution)/shard_map/all_to_all | solution.py:81
  22.5 1.0 copy-start.5
  32.9 12.8 %all-to-all-start = ((bf16[8,1,64,192]{3,2,1,0:T(8,128)(2,1)}), bf16[8,1,64,192]{3,2,1,0:T(8,128)(2,1)S(1)}, u32[]{:S(2)}, u32[]{:S(2)}) async-start(bf16[8,1,64,192]{3,2,1,0:T(8,128)(2,1)} %get-tuple-element.15), calls=%async_computation | async-start | bytes 524288 | tf_op jit(solution)/shard_map/all_to_all | solution.py:82
  36.3 43.6 %reduce-scatter.2.cloned.1.call-start = ((), (), s32[]{:S(2)}) async-start(), calls=%async_computation.4 | async-start | bytes 1966080 | tf_op jit(solution)/shard_map/reduce_scatter | solution.py:111
  50.7 95.8 %all-gather.9.cloned.1.call-start = ((), (), s32[]{:S(2)}) async-start(), calls=%async_computation.7 | async-start | bytes 1966080 | tf_op jit(solution)/shard_map/all_gather | solution.py:130
  50.8 2.0 copy-start.11
  79.9 22.3 %copy-start.13 = (s32[4]{0:T(128)S(1)}, s32[4]{0:T(128)}, u32[]{:S(2)}) copy-start(s32[4]{0:T(128)} %param.24) | copy-start | bytes 52
  79.9 22.5 %copy-start.9 = (s32[8,128]{1,0:T(8,128)S(1)}, s32[8,128]{1,0:T(8,128)}, u32[]{:S(2)}) copy-start(s32[8,128]{1,0:T(8,128)} %param.23) | copy-start | bytes 12292
  79.9 25.0 %copy-start.6 = (bf16[256,512]{1,0:T(8,128)(2,1)S(1)}, bf16[256,512]{1,0:T(8,128)(2,1)}, u32[]{:S(2)}) copy-start(bf16[256,512]{1,0:T(8,128)(2,1)} %param.18) | copy-start | bytes 786436
  81.4 24.1 %copy-start.7 = (bf16[48,512]{1,0:T(8,128)(2,1)S(1)}, bf16[48,512]{1,0:T(8,128)(2,1)}, u32[]{:S(2)}) copy-start(bf16[48,512]{1,0:T(8,128)(2,1)} %param.19) | copy-start | bytes 147460
  81.4 47.3 %copy-start.8 = (bf16[48,512]{1,0:T(8,128)(2,1)S(1)}, bf16[48,512]{1,0:T(8,128)(2,1)}, u32[]{:S(2)}) copy-start(bf16[48,512]{1,0:T(8,128)(2,1)} %param.20) | copy-start | bytes 147460
  101.4 77.7 %all-gather.7.cloned.1.call-start = ((), (), s32[]{:S(2)}) async-start(), calls=%async_computation.6 | async-start | bytes 4456448 | tf_op jit(solution)/shard_map/all_gather | solution.py:182
  102.2 106.0 %all-gather.5.cloned.1.call-start = ((), (), s32[]{:S(2)}) async-start(), calls=%async_computation.5 | async-start | bytes 1310720 | tf_op jit(solution)/shard_map/all_gather | solution.py:179
  102.7 43.6 %collective-permute-start.1 = (bf16[1,256]{1,0:T(2,128)(2,1)S(1)}, bf16[1,256]{1,0:T(2,128)(2,1)S(1)}, u32[]{:S(2)}, u32[]{:S(2)}) collective-permute-start(bf16[1,256]{1,0:T(2,128)(2,1)S(1)} %slice_convert_fusion), channel_id=1, source_target_pairs={{0,4},{4,8},{8,12},{12,16},{16,20},{20,24},{24,28},{28,32},{32,36}... | collective-permute-start | bytes 1544 | tf_op jit(solution)/shard_map/ppermute | solution.py:17
  105.0 41.5 %copy-start.3 = (bf16[4,64,4,128]{3,2,1,0:T(4,128)(2,1)}, bf16[4,64,4,128]{3,2,1,0:T(4,128)(2,1)S(1)}, u32[]{:S(2)}) copy-start(bf16[4,64,4,128]{3,2,1,0:T(4,128)(2,1)S(1)} %reshape.317) | copy-start | bytes 786436
  153.6 1.3 copy-start.2
  155.9 13.6 %collective-permute-start = (bf16[1,256,1024]{1,2,0:T(8,128)(2,1)}, bf16[1,256,1024]{1,2,0:T(8,128)(2,1)}, u32[]{:S(2)}, u32[]{:S(2)}) collective-permute-start(bf16[1,256,1024]{1,2,0:T(8,128)(2,1)} %copy.63), channel_id=1, source_target_pairs={{0,4},{4,8},{8,12},{12,16},{16,20},{20,24},{24,28},{28,32},{32,36}... | collective-permute-start | bytes 1572872 | tf_op jit(solution)/shard_map/ppermute | solution.py:17
  159.6 1.4 slice-start
  163.6 8.1 %slice-start.1 = ((bf16[4,64,4,128]{3,2,1,0:T(4,128)(2,1)}), bf16[4,63,4,128]{3,2,1,0:T(4,128)(2,1)S(1)}, s32[]{:S(2)}) async-start(bf16[4,64,4,128]{3,2,1,0:T(4,128)(2,1)} %copy-done.3), calls=%async_computation.9 | async-start | bytes 516096 | tf_op jit(solution)/shard_map/slice | solution.py:165
  171.7 1.3 copy-start.4
  172.9 35.2 %copy-start.12 = (bf16[256,1024]{1,0:T(8,128)(2,1)S(1)}, bf16[256,1024]{1,0:T(8,128)(2,1)}, u32[]{:S(2)}) copy-start(bf16[256,1024]{1,0:T(8,128)(2,1)} %param.17) | copy-start | bytes 1572868
Sparse Core Ops, SparseCore 0:
  50.8 29.0 reduce-scatter.1
  101.6 30.1 all-gather.8
  133.9 45.1 all-gather.6
  181.1 27.0 all-gather.4
where the time goes:
time: 220 us; the launch traced here: 219 us
  waiting for transfers between devices  82.3 us (37%)
  blocking collectives  59.2 us (27%)
  starting transfers between devices  18.7 us (8%)
  matrix products  17.6 us (8%)
  local copies, waits for them, and re-layouts  17 us (8%)
  between operations  13.6 us (6%)
  other arithmetic  10.8 us (5%)
    all_gather x1, waiting for transfers between devices, per_device(): all_heads = lax.all_gather(attended, 'tp', axis=1, tiled=True)  29.1 us
    reduce_scatter x1, waiting for transfers between devices, per_device(): lax.psum_scatter(term.astype(jnp.bfloat16), 'tp', scatter_dimension=0, ti...  27.2 us
    all_gather x1, blocking collectives, per_device(): lax.all_gather(key_weight_matrix, 'ctx', axis=0, tiled=True)  23.3 us
    all_to_all x1, blocking collectives, per_device(): lax.all_to_all(encoded.reshape(owners, per_owner, quarter, enc_width), 'n...  18.6 us
    all_gather x1, blocking collectives, per_device(): lax.all_gather(value_weight_matrix, 'ctx', axis=0, tiled=True)  17.3 us
    all_to_all x1, starting transfers between devices, per_device(): lax.all_to_all(sent_keys, 'nbr', split_axis=0, concat_axis=0, tiled=True)  10.9 us
    all_to_all x1, waiting for transfers between devices, per_device(): lax.all_to_all(sent_keys, 'nbr', split_axis=0, concat_axis=0, tiled=True)  8.67 us
    all_to_all x1, waiting for transfers between devices, per_device(): lax.all_to_all(sent_values, 'nbr', split_axis=0, concat_axis=0, tiled=True)  7.43 us
  transfers between devices with their start and end apart: 8, of which 6 were waited for; matrix products, arithmetic and copies ran while one was open for 12% of the time, Pallas kernels for 0%

commit v1 on v0

--- a/solution.py
+++ b/solution.py
@@ -176,7 +176,9 @@
         score_scale,
     )
     attended = jnp.concatenate([early_rows, last_rows], axis=1).reshape(tok_rows, head_cols)
-    all_heads = lax.all_gather(attended, "tp", axis=1, tiled=True)
+    all_heads = jnp.concatenate(
+        lax.all_to_all(jnp.stack([attended] * lax.axis_size("tp")), "tp", 0, 0), axis=1
+    )
     mixed_out = jnp.dot(
         all_heads,
         lax.all_gather(w_out, "ctx", axis=0, tiled=True),

time: 220 us -> 209 us (0.950)
  the two profiles are of different devices: /device:TPU:1 before, /device:TPU:8 now
where the time goes in v1:
time: 209 us
  blocking collectives  70.9 us (34%)
  waiting for transfers between devices  61 us (29%)
  starting transfers between devices  18.2 us (9%)
  matrix products  17.3 us (8%)
  local copies, waits for them, and re-layouts  16.8 us (8%)
  between operations  13.6 us (7%)
  other arithmetic  10.8 us (5%)
    reduce_scatter x1, waiting for transfers between devices, per_device(): lax.psum_scatter(term.astype(jnp.bfloat16), 'tp', scatter_dimension=0, ti...  25.2 us
    all_to_all x1, blocking collectives, per_device(): lax.all_to_all(encoded.reshape(owners, per_owner, quarter, enc_width), 'n...  20.9 us
    all_gather x1, blocking collectives, per_device(): lax.all_gather(value_weight_matrix, 'ctx', axis=0, tiled=True)  18.1 us
    all_gather x1, blocking collectives, per_device(): lax.all_gather(key_weight_matrix, 'ctx', axis=0, tiled=True)  17.9 us
    ppermute x2, waiting for transfers between devices, from_behind(): return lax.ppermute(block, axis, route)  16.4 us
    all_to_all x1, blocking collectives, per_device(): lax.all_to_all(jnp.stack([attended] * lax.axis_size('tp')), 'tp', 0, 0)  14.1 us
    all_to_all x1, starting transfers between devices, per_device(): lax.all_to_all(sent_keys, 'nbr', split_axis=0, concat_axis=0, tiled=True)  10.3 us
    all_to_all x1, waiting for transfers between devices, per_device(): lax.all_to_all(sent_keys, 'nbr', split_axis=0, concat_axis=0, tiled=True)  10.2 us
  transfers between devices with their start and end apart: 7, of which 4 were waited for; matrix products, arithmetic and copies ran while one was open for 12% of the time, Pallas kernels for 0%

profile of v1, /device:TPU:8, one launch (start us, length us, event | category | flops | bytes accessed | tf_op | source)
XLA Modules:
  0.0 208.6 jit_solution(2813125105863374847)
XLA Ops:
  6.5 1.0 dynamic-slice_reduce_fusion
  7.6 1.0 copy.54
  8.6 1.0 copy.57
  9.6 0.6 gather_fusion.1
  10.2 0.6 gather_fusion.2
  10.7 0.9 fusion.37
  11.7 10.3 %all-to-all-start.1 = ((bf16[8,1,64,192]{3,2,1,0:T(8,128)(2,1)}), bf16[8,1,64,192]{3,2,1,0:T(8,128)(2,1)S(1)}, u32[]{:S(2)}, u32[]{:S(2)}) async-start(bf16[8,1,64,192]{3,2,1,0:T(8,128)(2,1)} %get-tuple-element.14), calls=%async_computation.1 | async-start | bytes 524288 | tf_op jit(solution)/shard_map/all_to_all | solution.py:81
  22.0 0.4 multiply_reduce_fusion
  22.4 0.4 multiply_convert_fusion
  22.8 0.1 copy-done.5
  22.9 0.7 fusion.20
  23.7 10.2 %all-to-all-done.1 = bf16[8,1,64,192]{3,2,1,0:T(8,128)(2,1)S(1)} async-done(((bf16[8,1,64,192]{3,2,1,0:T(8,128)(2,1)}), bf16[8,1,64,192]{3,2,1,0:T(8,128)(2,1)S(1)}, u32[]{:S(2)}, u32[]{:S(2)}) %all-to-all-start.1) | async-done | bytes 196640 | tf_op jit(solution)/shard_map/all_to_all | solution.py:81
  33.9 3.4 %all-to-all-start = ((bf16[8,1,64,192]{3,2,1,0:T(8,128)(2,1)}), bf16[8,1,64,192]{3,2,1,0:T(8,128)(2,1)S(1)}, u32[]{:S(2)}, u32[]{:S(2)}) async-start(bf16[8,1,64,192]{3,2,1,0:T(8,128)(2,1)} %get-tuple-element.15), calls=%async_computation | async-start | bytes 524288 | tf_op jit(solution)/shard_map/all_to_all | solution.py:82
  37.3 0.2 copy.59
  37.5 0.5 fusion.67
  38.0 1.2 convolution_multiply_fusion.1
  39.2 8.5 %all-to-all-done = bf16[8,1,64,192]{3,2,1,0:T(8,128)(2,1)S(1)} async-done(((bf16[8,1,64,192]{3,2,1,0:T(8,128)(2,1)}), bf16[8,1,64,192]{3,2,1,0:T(8,128)(2,1)S(1)}, u32[]{:S(2)}, u32[]{:S(2)}) %all-to-all-start) | async-done | bytes 196640 | tf_op jit(solution)/shard_map/all_to_all | solution.py:82
  47.7 0.2 copy.56
  47.9 1.7 fusion.21
  49.6 0.7 copy.62
  50.3 0.7 reshape.314
  51.0 1.7 convolution_convert_fusion.1
  52.8 2.0 convert_element_type.61
  54.7 25.2 %reduce-scatter.2.cloned.1.call-done = bf16[256,768]{1,0:T(8,128)(2,1)} async-done(((bf16[1024,768]{1,0:T(8,128)(2,1)}), bf16[256,768]{1,0:T(8,128)(2,1)}) %reduce-scatter.2.cloned.1.call-update) | async-done | bytes 393232 | tf_op jit(solution)/shard_map/reduce_scatter | solution.py:111
  80.0 1.5 multiply_reduce_fusion.1
  81.5 1.4 fusion.33
  82.9 20.9 %all_to_all.20 = bf16[8,1,32,768]{3,2,1,0:T(8,128)(2,1)} all-to-all(bf16[8,1,32,768]{3,2,1,0:T(8,128)(2,1)S(1)} %fusion.33), channel_id=1, replica_groups=mesh['ctx'=16,'nbr'=8,'tp'=4] {'nbr'}, dimensions={0} | all-to-all | bytes 786432 | tf_op jit(solution)/shard_map/all_to_all | solution.py:122
  103.9 0.7 all-gather.4.cloned.1.call-update
  104.7 0.1 lt.62
  104.8 0.2 and_reduce_fusion
  105.1 2.5 %collective-permute-start.1 = (bf16[1,256]{1,0:T(2,128)(2,1)S(1)}, bf16[1,256]{1,0:T(2,128)(2,1)S(1)}, u32[]{:S(2)}, u32[]{:S(2)}) collective-permute-start(bf16[1,256]{1,0:T(2,128)(2,1)S(1)} %slice_convert_fusion), channel_id=1, source_target_pairs={{0,4},{4,8},{8,12},{12,16},{16,20},{20,24},{24,28},{28,32},{32,36}... | collective-permute-start | bytes 1544 | tf_op jit(solution)/shard_map/ppermute | solution.py:17
  107.7 0.1 select_reduce_fusion.2
  107.8 0.1 reduce_sum.64
  107.9 0.1 copy.70
  108.2 17.9 %all_gather.13 = bf16[768,512]{1,0:T(8,128)(2,1)S(1)} all-gather(bf16[48,512]{1,0:T(8,128)(2,1)S(1)} %copy-done.7), channel_id=1, replica_groups=mesh['ctx'=16,'nbr'=8,'tp'=4] {'ctx'}, dimensions={0}, use_global_device_ids=true | all-gather | bytes 835584 | tf_op jit(solution)/shard_map/all_gather | solution.py:118
  126.0 18.1 %all_gather.14 = bf16[768,512]{1,0:T(8,128)(2,1)S(1)} all-gather(bf16[48,512]{1,0:T(8,128)(2,1)S(1)} %copy-done.8), channel_id=1, replica_groups=mesh['ctx'=16,'nbr'=8,'tp'=4] {'ctx'}, dimensions={0}, use_global_device_ids=true | all-gather | bytes 835584 | tf_op jit(solution)/shard_map/all_gather | solution.py:119
  144.1 0.1 reduce_or.27
  144.2 0.1 reduce_or.28
  144.3 0.1 fusion.66
  144.5 4.5 %convolution_convert_fusion = bf16[8,128,1024]{2,1,0:T(8,128)(2,1)} fusion(bf16[768,512]{1,0:T(8,128)(2,1)S(1)} %all_gather.14, bf16[768,512]{1,0:T(8,128)(2,1)S(1)} %all_gather.13, bf16[8,1,128,768]{3,2,0,1:T(8,128)(2,1)} %all-gather.6.cloned.1.call-done), kind=kOutput, calls=%fused_computation.12 | convolution fusion | flops 1614807040 | bytes 5242880 | tf_op jit(solution)/shard_map/dot_general | solution.py:129
  149.0 2.3 %gather_fusion = bf16[8,128,1024]{2,1,0:T(8,128)(2,1)S(1)} fusion(bf16[8,128,1024]{2,1,0:T(8,128)(2,1)} %convolution_convert_fusion, s32[1024]{0:T(1024)S(1)} %pad_clamp_fusion), kind=kCustom, calls=%fused_computation.2 | custom fusion | bytes 4194336 | tf_op jit(solution)/shard_map/jit(_take)/gather | solution.py:138
  151.3 0.3 broadcast_select_fusion
  151.6 1.3 copy-done.2
  152.9 1.0 copy.65
  153.9 1.9 collective-permute-start
  155.8 0.3 bitcast_select_fusion
  156.1 1.3 slice_bitcast_fusion
  157.4 0.4 fusion.27
  157.7 0.2 fusion.70
  158.0 0.1 fusion.49
  158.1 0.7 slice-done
  158.8 0.7 copy.66
  159.5 1.5 copy.83
  161.0 0.4 fusion.40
  161.4 16.4 %collective-permute-done = bf16[1,256,1024]{1,2,0:T(8,128)(2,1)} collective-permute-done((bf16[1,256,1024]{1,2,0:T(8,128)(2,1)}, bf16[1,256,1024]{1,2,0:T(8,128)(2,1)}, u32[]{:S(2)}, u32[]{:S(2)}) %collective-permute-start) | collective-permute-done | bytes 524320 | tf_op jit(solution)/shard_map/ppermute | solution.py:17
  177.8 2.1 %pad_maximum_fusion = (bf16[4,256,512]{1,2,0:T(8,128)(2,1)S(1)}, bf16[4,256,512]{1,2,0:T(8,128)(2,1)}) fusion(bf16[3,256,1024]{1,2,0:T(8,128)(2,1)S(1)} %copy.66, bf16[1,256,1024]{1,2,0:T(8,128)(2,1)} %collective-permute-done), kind=kLoop, calls=%fused_computation.44 | loop fusion | flops 4194304 | bytes 4194304 | tf_op jit(solution)/shard_map/concatenate | solution.py:161
  179.9 0.3 convolution_multiply_fusion
  180.2 0.4 fusion.71
  180.7 0.5 copy-done.4
  181.1 1.8 fusion.22
  183.0 0.3 copy.84
  183.4 0.3 reshape.370
  183.8 14.1 %all_to_all.21 = bf16[4,256,512]{1,2,0:T(8,128)(2,1)S(1)} all-to-all(bf16[4,256,512]{1,2,0:T(8,128)(2,1)S(1)} %stack.3), channel_id=1, replica_groups=mesh['ctx'=16,'nbr'=8,'tp'=4] {'tp'}, dimensions={0} | all-to-all | bytes 2097152 | tf_op jit(solution)/shard_map/all_to_all | solution.py:180
  197.8 4.3 %fusion.18 = bf16[256,1024]{1,0:T(8,128)(2,1)} fusion(bf16[256,2048]{0,1:T(8,128)(2,1)S(1)} %bitcast.151, bf16[2048,1024]{1,0:T(8,128)(2,1)} %all-gather.4.cloned.1.call-done, bf16[256,1024]{1,0:T(8,128)(2,1)S(1)} %copy-done.12), kind=kOutput, calls=%fused_computation.27 | convolution fusion | flops 1074528256 | bytes 6291456 | tf_op jit(solution)/shard_map/dot_general | solution.py:182
  (68 shorter events, 1.2 us)
Async XLA Ops:
  6.5 44.5 %copy-start = (bf16[192,768]{1,0:T(8,128)(2,1)S(1)}, bf16[192,768]{1,0:T(8,128)(2,1)}, u32[]{:S(2)}) copy-start(bf16[192,768]{1,0:T(8,128)(2,1)} %param.30) | copy-start | bytes 884740
  6.5 15.4 %copy-start.1 = (bf16[8,128,768]{2,1,0:T(8,128)(2,1)S(1)}, bf16[8,128,768]{2,1,0:T(8,128)(2,1)}, u32[]{:S(2)}) copy-start(bf16[8,128,768]{2,1,0:T(8,128)(2,1)} %param.22) | copy-start | bytes 4718596
  9.6 12.8 %copy-start.10 = (bf16[768]{0:T(1024)(128)(2,1)S(1)}, bf16[768]{0:T(1024)(128)(2,1)}, u32[]{:S(2)}) copy-start(bf16[768]{0:T(1024)(128)(2,1)} %param.28) | copy-start | bytes 4612
  11.7 22.2 %all-to-all-start.1 = ((bf16[8,1,64,192]{3,2,1,0:T(8,128)(2,1)}), bf16[8,1,64,192]{3,2,1,0:T(8,128)(2,1)S(1)}, u32[]{:S(2)}, u32[]{:S(2)}) async-start(bf16[8,1,64,192]{3,2,1,0:T(8,128)(2,1)} %get-tuple-element.14), calls=%async_computation.1 | async-start | bytes 524288 | tf_op jit(solution)/shard_map/all_to_all | solution.py:81
  22.0 1.0 copy-start.5
  33.9 13.8 %all-to-all-start = ((bf16[8,1,64,192]{3,2,1,0:T(8,128)(2,1)}), bf16[8,1,64,192]{3,2,1,0:T(8,128)(2,1)S(1)}, u32[]{:S(2)}, u32[]{:S(2)}) async-start(bf16[8,1,64,192]{3,2,1,0:T(8,128)(2,1)} %get-tuple-element.15), calls=%async_computation | async-start | bytes 524288 | tf_op jit(solution)/shard_map/all_to_all | solution.py:82
  37.3 42.7 %reduce-scatter.2.cloned.1.call-start = ((), (), s32[]{:S(2)}) async-start(), calls=%async_computation.5 | async-start | bytes 1966080 | tf_op jit(solution)/shard_map/reduce_scatter | solution.py:111
  52.7 91.7 %all-gather.6.cloned.1.call-start = ((), (), s32[]{:S(2)}) async-start(), calls=%async_computation.7 | async-start | bytes 1966080 | tf_op jit(solution)/shard_map/all_gather | solution.py:130
  52.8 2.0 copy-start.11
  80.0 24.6 %copy-start.13 = (s32[4]{0:T(128)S(1)}, s32[4]{0:T(128)}, u32[]{:S(2)}) copy-start(s32[4]{0:T(128)} %param.24) | copy-start | bytes 52
  80.0 24.8 %copy-start.9 = (s32[8,128]{1,0:T(8,128)S(1)}, s32[8,128]{1,0:T(8,128)}, u32[]{:S(2)}) copy-start(s32[8,128]{1,0:T(8,128)} %param.23) | copy-start | bytes 12292
  80.0 27.6 %copy-start.6 = (bf16[256,512]{1,0:T(8,128)(2,1)S(1)}, bf16[256,512]{1,0:T(8,128)(2,1)}, u32[]{:S(2)}) copy-start(bf16[256,512]{1,0:T(8,128)(2,1)} %param.18) | copy-start | bytes 786436
  81.5 26.7 %copy-start.7 = (bf16[48,512]{1,0:T(8,128)(2,1)S(1)}, bf16[48,512]{1,0:T(8,128)(2,1)}, u32[]{:S(2)}) copy-start(bf16[48,512]{1,0:T(8,128)(2,1)} %param.19) | copy-start | bytes 147460
  81.5 44.5 %copy-start.8 = (bf16[48,512]{1,0:T(8,128)(2,1)S(1)}, bf16[48,512]{1,0:T(8,128)(2,1)}, u32[]{:S(2)}) copy-start(bf16[48,512]{1,0:T(8,128)(2,1)} %param.20) | copy-start | bytes 147460
  103.9 94.0 %all-gather.4.cloned.1.call-start = ((), (), s32[]{:S(2)}) async-start(), calls=%async_computation.6 | async-start | bytes 4456448 | tf_op jit(solution)/shard_map/all_gather | solution.py:184
  105.1 39.2 %collective-permute-start.1 = (bf16[1,256]{1,0:T(2,128)(2,1)S(1)}, bf16[1,256]{1,0:T(2,128)(2,1)S(1)}, u32[]{:S(2)}, u32[]{:S(2)}) collective-permute-start(bf16[1,256]{1,0:T(2,128)(2,1)S(1)} %slice_convert_fusion), channel_id=1, source_target_pairs={{0,4},{4,8},{8,12},{12,16},{16,20},{20,24},{24,28},{28,32},{32,36}... | collective-permute-start | bytes 1544 | tf_op jit(solution)/shard_map/ppermute | solution.py:17
  107.7 36.8 %copy-start.3 = (bf16[4,64,4,128]{3,2,1,0:T(4,128)(2,1)}, bf16[4,64,4,128]{3,2,1,0:T(4,128)(2,1)S(1)}, u32[]{:S(2)}) copy-start(bf16[4,64,4,128]{3,2,1,0:T(4,128)(2,1)S(1)} %reshape.322) | copy-start | bytes 786436
  151.5 1.3 copy-start.2
  153.9 23.8 %collective-permute-start = (bf16[1,256,1024]{1,2,0:T(8,128)(2,1)}, bf16[1,256,1024]{1,2,0:T(8,128)(2,1)}, u32[]{:S(2)}, u32[]{:S(2)}) collective-permute-start(bf16[1,256,1024]{1,2,0:T(8,128)(2,1)} %copy.65), channel_id=1, source_target_pairs={{0,4},{4,8},{8,12},{12,16},{16,20},{20,24},{24,28},{28,32},{32,36}... | collective-permute-start | bytes 1572872 | tf_op jit(solution)/shard_map/ppermute | solution.py:17
  157.4 1.4 slice-start
  161.4 18.5 %slice-start.1 = ((bf16[4,64,4,128]{3,2,1,0:T(4,128)(2,1)}), bf16[4,63,4,128]{3,2,1,0:T(4,128)(2,1)S(1)}, s32[]{:S(2)}) async-start(bf16[4,64,4,128]{3,2,1,0:T(4,128)(2,1)} %copy-done.3), calls=%async_computation.9 | async-start | bytes 516096 | tf_op jit(solution)/shard_map/slice | solution.py:165
  179.9 1.2 copy-start.4
  183.4 14.5 %copy-start.12 = (bf16[256,1024]{1,0:T(8,128)(2,1)S(1)}, bf16[256,1024]{1,0:T(8,128)(2,1)}, u32[]{:S(2)}) copy-start(bf16[256,1024]{1,0:T(8,128)(2,1)} %param.17) | copy-start | bytes 1572868
Sparse Core Ops, SparseCore 0:
  52.8 27.1 reduce-scatter.1
  104.0 26.8 all-gather.5
  133.0 44.5 all-gather.3
